TPU v7x, 128 devices: a whole 4x4x4 slice. The times are simulated.
128 devices in a mesh: gx: 4 (over y_hi, core), gy: 4 (over z), gz: 8 (over y_lo, x).
Axes of the slice: x: 4, y: 4 (y_hi: 2, y_lo: 2; y = y_hi * 2 + y_lo), z: 4, core: 2. Of those that a mesh axis runs over, the one named last changes fastest.
Arguments:
- block_in: bfloat16 [768, 8192], P(('gy', 'gz'), 'gx'), may hold values from -6 to 6
- online_gate: bfloat16 [8192, 16384], P('gx', ('gy', 'gz')), may hold values from -6 to 6
- online_up: bfloat16 [8192, 16384], P('gx', ('gy', 'gz')), may hold values from -6 to 6
- online_down: bfloat16 [16384, 8192], P(('gy', 'gz'), 'gx'), may hold values from -6 to 6
- target_gate: bfloat16 [8192, 16384], P('gx', ('gy', 'gz')), may hold values from -6 to 6
- target_up: bfloat16 [8192, 16384], P('gx', ('gy', 'gz')), may hold values from -6 to 6
- target_down: bfloat16 [16384, 8192], P(('gy', 'gz'), 'gx'), may hold values from -6 to 6
- cotangent: bfloat16 [768, 8192], P(('gy', 'gz'), 'gx'), may hold values from -6 to 6
Outputs:
- online_out: bfloat16 [768, 8192], P(('gy', 'gz'), 'gx')
- target_out: bfloat16 [768, 8192], P(('gy', 'gz'), 'gx')
- grad_in: bfloat16 [768, 8192], P(('gy', 'gz'), 'gx')
- grad_gate: bfloat16 [8192, 16384], P('gx', ('gy', 'gz'))
- grad_up: bfloat16 [8192, 16384], P('gx', ('gy', 'gz'))
- grad_down: bfloat16 [16384, 8192], P(('gy', 'gz'), 'gx')
- new_gate: bfloat16 [8192, 16384], P('gx', ('gy', 'gz'))
- new_up: bfloat16 [8192, 16384], P('gx', ('gy', 'gz'))
- new_down: bfloat16 [16384, 8192], P(('gy', 'gz'), 'gx')
All inputs are finite; a program needn't handle non-finite values.
Results may differ from a plain program's by a relative error of at most 0.0049.
Values may be sent and summed in bfloat16 or wider, within the bound.
No kernel may reach another device: no remote copies, remote signals or barrier semaphores. Data moves between devices by JAX's collectives and lax.ppermute only.
A program may use at most 128 MiB of HBM per device.

v0:
```python
import math

import jax
import jax.numpy as jnp
from jax import lax
from jax.sharding import PartitionSpec as P

D = 8192
FF = 16384


POLYAK = 0.05


def activate(pre_gate, pre_up):
    return (jax.nn.silu(pre_gate) * pre_up).astype(jnp.bfloat16)


def hidden_grads(pre_gate, pre_up, hidden_grad):
    sigmoid_value = jax.nn.sigmoid(pre_gate)
    d_up = (hidden_grad * pre_gate * sigmoid_value).astype(jnp.bfloat16)
    d_gate = (
        hidden_grad * pre_up * sigmoid_value * (1.0 + pre_gate * (1.0 - sigmoid_value))
    ).astype(jnp.bfloat16)
    return (d_gate, d_up)


def blend(online, target):
    online_f = online.astype(jnp.float32)
    target_f = target.astype(jnp.float32)
    return (target_f + POLYAK * (online_f - target_f)).astype(jnp.bfloat16)


def on_device(
    block_in, online_gate, online_up, online_down, target_gate, target_up, target_down, cotangent
):
    scale_in = 1.0 / math.sqrt(D)
    scale_hid = 1.0 / math.sqrt(FF)
    rows_all, cot_all = (
        lax.all_gather(block_in, ("gy", "gz"), axis=0, tiled=True),
        lax.all_gather(cotangent, ("gy", "gz"), axis=0, tiled=True),
    )

    def project(weight):
        return jnp.dot(rows_all, weight, preferred_element_type=jnp.float32) * scale_in

    partial_on_gate = project(online_gate)
    partial_on_up = project(online_up)
    partial_tg_gate = project(target_gate)
    partial_tg_up = project(target_up)
    hidden_part = (
        jnp.einsum("tk,fk->tf", cot_all, online_down, preferred_element_type=jnp.float32)
        * scale_hid
    )
    on_gate, on_up, tg_gate, tg_up = lax.psum(
        (partial_on_gate, partial_on_up, partial_tg_gate, partial_tg_up), "gx"
    )
    on_hidden = activate(on_gate, on_up)
    tg_hidden = activate(tg_gate, tg_up)
    hidden_grad = lax.psum(hidden_part, "gx")
    d_gate, d_up = hidden_grads(on_gate, on_up, hidden_grad)
    row_slice = on_hidden
    online_out = lax.psum_scatter(
        jnp.dot(row_slice, online_down, preferred_element_type=jnp.float32) * scale_hid,
        ("gy", "gz"),
        scatter_dimension=0,
        tiled=True,
    ).astype(jnp.bfloat16)
    row_slice = tg_hidden
    target_out = lax.psum_scatter(
        jnp.dot(row_slice, target_down, preferred_element_type=jnp.float32) * scale_hid,
        ("gy", "gz"),
        scatter_dimension=0,
        tiled=True,
    ).astype(jnp.bfloat16)
    summed = jnp.einsum("tf,kf->tk", d_gate, online_gate, preferred_element_type=jnp.float32)
    summed = summed + jnp.einsum("tf,kf->tk", d_up, online_up, preferred_element_type=jnp.float32)
    grad_in = lax.psum_scatter(
        summed * scale_in, ("gy", "gz"), scatter_dimension=0, tiled=True
    ).astype(jnp.bfloat16)
    grad_gate = (
        jnp.einsum("tk,tf->kf", rows_all, d_gate, preferred_element_type=jnp.float32) * scale_in
    ).astype(jnp.bfloat16)
    grad_up = (
        jnp.einsum("tk,tf->kf", rows_all, d_up, preferred_element_type=jnp.float32) * scale_in
    ).astype(jnp.bfloat16)
    grad_down = (
        jnp.einsum("tf,tk->fk", on_hidden, cot_all, preferred_element_type=jnp.float32) * scale_hid
    ).astype(jnp.bfloat16)
    new_gate = blend(online_gate, target_gate)
    new_up = blend(online_up, target_up)
    new_down = blend(online_down, target_down)
    return (
        online_out,
        target_out,
        grad_in,
        grad_gate,
        grad_up,
        grad_down,
        new_gate,
        new_up,
        new_down,
    )


def solution(mesh):
    placed = (
        P(("gy", "gz"), "gx"),
        P("gx", ("gy", "gz")),
        P("gx", ("gy", "gz")),
        P(("gy", "gz"), "gx"),
        P("gx", ("gy", "gz")),
        P("gx", ("gy", "gz")),
        P(("gy", "gz"), "gx"),
        P(("gy", "gz"), "gx"),
    )
    return jax.shard_map(
        on_device,
        mesh=mesh,
        in_specs=placed,
        out_specs=(
            P(("gy", "gz"), "gx"),
            P(("gy", "gz"), "gx"),
            P(("gy", "gz"), "gx"),
            P("gx", ("gy", "gz")),
            P("gx", ("gy", "gz")),
            P(("gy", "gz"), "gx"),
            P("gx", ("gy", "gz")),
            P("gx", ("gy", "gz")),
            P(("gy", "gz"), "gx"),
        ),
        check_vma=False,
    )
```

profile of v0, /device:TPU:10, one launch (start us, length us, event | category | flops | bytes accessed | tf_op | source)
XLA Modules:
  0.0 1006.1 jit_solution(4394620310255874634)
XLA Ops:
  7.2 0.7 all-gather.3.cloned.1.call-update
  8.0 0.7 all-gather.5.cloned.1.call-update
  8.7 152.3 %all-gather.3.cloned.1.call-done = bf16[768,2048]{1,0:T(8,128)(2,1)} async-done(((bf16[24,2048]{1,0:T(8,128)(2,1)}), bf16[768,2048]{1,0:T(8,128)(2,1)}) %all-gather.3.cloned.1.call-update) | async-done | bytes 3145744 | tf_op jit(solution)/shard_map/all_gather | solution.py:40
  161.0 5.6 convolution_multiply_fusion.3
  166.6 4.7 convolution_multiply_fusion.4
  171.3 3.0 convolution_multiply_fusion.5
  174.2 3.0 convolution_multiply_fusion.6
  177.2 140.8 %all-gather.5.cloned.1.call-done = bf16[768,2048]{1,0:T(8,128)(2,1)} async-done(((bf16[24,2048]{1,0:T(8,128)(2,1)}), bf16[768,2048]{1,0:T(8,128)(2,1)}) %all-gather.5.cloned.1.call-update) | async-done | bytes 3145744 | tf_op jit(solution)/shard_map/all_gather | solution.py:41
  318.0 5.5 convolution_multiply_fusion.2
  323.5 0.0 reduce-scatter.6.cloned.1.call-start
  323.5 158.6 %all-reduce.3.cloned.1.call-done = (f32[768,512]{1,0:T(8,128)}, f32[768,512]{1,0:T(8,128)}, f32[768,512]{1,0:T(8,128)}, f32[768,512]{1,0:T(8,128)}, f32[768,512]{1,0:T(8,128)}) async-done(((f32[768,512]{1,0:T(8,128)}, f32[768,512]{1,0:T(8,128)}, f32[768,512]{1,0:T(8,128)}, f32[768,512]{1,0:T(8,128)}, f32[768,512]{1,0:T(8,128)}), (f32[768,512]{1,0:T(8,128)}, f32[768,512]{1,0:T(8,128)}, f32[768,512]{1,0:T(8,128)}, ...) | async-done | bytes 7864336 | tf_op jit(solution)/shard_map/psum | solution.py:55
  482.2 7.0 convolution_multiply_fusion
  489.2 0.0 reduce-scatter.4.cloned.1.call-start
  489.3 4.6 multiply_convert_fusion.3
  493.9 0.9 copy-done.8
  494.8 4.4 convolution_multiply_fusion.1
  499.2 0.2 reduce-scatter.8.cloned.1.call-start
  499.5 3.8 fusion.10
  503.3 4.4 add_multiply_fusion
  507.8 4.7 fusion.5
  512.5 5.2 fusion.1
  517.8 3.2 fusion.6
  520.9 3.9 copy.17
  524.8 4.3 fusion.7
  529.1 4.0 copy.18
  533.1 5.1 multiply_convert_fusion
  538.2 113.4 %reduce-scatter.6.cloned.1.call-done = f32[24,2048]{1,0:T(8,128)} async-done(((f32[768,2048]{1,0:T(8,128)}), f32[24,2048]{1,0:T(8,128)}) %reduce-scatter.6.cloned.1.call-update) | async-done | bytes 196624 | tf_op jit(solution)/shard_map/reduce_scatter | solution.py:70
  651.6 1.6 convert_element_type.66
  653.1 171.5 %reduce-scatter.4.cloned.1.call-done = f32[24,2048]{1,0:T(8,128)} async-done(((f32[768,2048]{1,0:T(8,128)}), f32[24,2048]{1,0:T(8,128)}) %reduce-scatter.4.cloned.1.call-update) | async-done | bytes 196624 | tf_op jit(solution)/shard_map/reduce_scatter | solution.py:63
  824.6 1.6 convert_element_type.64
  826.2 171.5 %reduce-scatter.8.cloned.1.call-done = f32[24,2048]{1,0:T(8,128)} async-done(((f32[768,2048]{1,0:T(8,128)}), f32[24,2048]{1,0:T(8,128)}) %reduce-scatter.8.cloned.1.call-update) | async-done | bytes 196624 | tf_op jit(solution)/shard_map/reduce_scatter | solution.py:78
  997.7 1.6 convert_element_type.69
  (30 shorter events, 0.2 us)
Async XLA Ops:
  7.2 153.8 %all-gather.3.cloned.1.call-start = ((), (), s32[]{:S(2)}) async-start(), calls=%async_computation.3 | async-start | bytes 3244032 | tf_op jit(solution)/shard_map/all_gather | solution.py:40
  7.9 310.1 %all-gather.5.cloned.1.call-start = ((), (), s32[]{:S(2)}) async-start(), calls=%async_computation.6 | async-start | bytes 3244032 | tf_op jit(solution)/shard_map/all_gather | solution.py:41
  8.7 473.5 %all-reduce.3.cloned.1.call-start = ((), (), s32[]{:S(2)}) async-start(), calls=%async_computation.8 | async-start | bytes 15728640 | tf_op jit(solution)/shard_map/psum | solution.py:55
  161.0 5.6 copy-start
  166.6 4.7 copy-start.3
  171.3 3.0 copy-start.6
  323.5 328.1 %reduce-scatter.6.cloned.1.call-start = ((), (), s32[]{:S(2)}) async-start(), calls=%async_computation.5 | async-start | bytes 6488064 | tf_op jit(solution)/shard_map/reduce_scatter | solution.py:70
  489.2 335.4 %reduce-scatter.4.cloned.1.call-start = ((), (), s32[]{:S(2)}) async-start(), calls=%async_computation.4 | async-start | bytes 6488064 | tf_op jit(solution)/shard_map/reduce_scatter | solution.py:63
  489.3 5.5 copy-start.2
  493.9 0.9 copy-start.8
  499.2 498.5 %reduce-scatter.8.cloned.1.call-start = ((), (), s32[]{:S(2)}) async-start(), calls=%async_computation.7 | async-start | bytes 6488064 | tf_op jit(solution)/shard_map/reduce_scatter | solution.py:78
  499.4 3.8 copy-start.1
  499.5 3.8 copy-start.4
  507.7 4.8 copy-start.5
  507.8 4.8 copy-start.7
  507.8 4.8 copy-start.11
  512.5 5.2 copy-start.10
  529.1 4.0 copy-start.9
Sparse Core Ops, SparseCore 0:
  9.7 151.2 all-gather.2
  162.6 155.3 all-gather.4
  323.6 158.5 all-reduce.2
  489.4 162.1 reduce-scatter.5
  653.8 170.7 reduce-scatter.3
  826.9 170.7 reduce-scatter.7
where the time goes:
time: 1020 us; the launch traced here: 1010 us
  waiting for transfers between devices  909 us (89%)
  matrix products  53.9 us (5%)
  other arithmetic  19.3 us (2%)
  between operations  14.2 us (1%)
    reduce_scatter x1, waiting for transfers between devices, on_device(): lax.psum_scatter(summed * scale_in, ('gy', 'gz'), scatter_dimension=0, ti...  171 us
    reduce_scatter x1, waiting for transfers between devices, on_device(): lax.psum_scatter(jnp.dot(row_slice, online_down, preferred_element_type=j...  171 us
    psum x1, waiting for transfers between devices, on_device(): lax.psum((partial_on_gate, partial_on_up, partial_tg_gate, partial_tg_up)...  159 us
    all_gather x1, waiting for transfers between devices, on_device(): lax.all_gather(block_in, ('gy', 'gz'), axis=0, tiled=True)  152 us
    all_gather x1, waiting for transfers between devices, on_device(): lax.all_gather(cotangent, ('gy', 'gz'), axis=0, tiled=True)  141 us
    reduce_scatter x1, waiting for transfers between devices, on_device(): lax.psum_scatter(jnp.dot(row_slice, target_down, preferred_element_type=j...  113 us
  transfers between devices with their start and end apart: 6, of which 6 were waited for; matrix products, arithmetic and copies ran while one was open for 7% of the time, Pallas kernels for 0%

commit v1 on v0

v1 whole, which is shorter than its diff:
```python
import math

import jax
import jax.numpy as jnp
from jax import lax
from jax.sharding import PartitionSpec as P

D = 8192
FF = 16384
POLYAK = 0.05
TOKENS = ("gy", "gz")
BF = jnp.bfloat16
F32 = jnp.float32


def activate(pre_gate, pre_up):
    return (jax.nn.silu(pre_gate) * pre_up).astype(BF)


def hidden_grads(pre_gate, pre_up, hidden_grad):
    sigmoid_value = jax.nn.sigmoid(pre_gate)
    d_up = (hidden_grad * pre_gate * sigmoid_value).astype(BF)
    d_gate = (
        hidden_grad * pre_up * sigmoid_value * (1.0 + pre_gate * (1.0 - sigmoid_value))
    ).astype(BF)
    return (d_gate, d_up)


def blend(online, target):
    online_f = online.astype(F32)
    target_f = target.astype(F32)
    return (target_f + POLYAK * (online_f - target_f)).astype(BF)


def gather_rows(rows):
    copies = jnp.broadcast_to(rows[None], (32,) + rows.shape)
    got = lax.all_to_all(copies, TOKENS, 0, 0)
    return got.reshape(32 * rows.shape[0], rows.shape[1])


def scatter_sum(part):
    chunks = part.reshape(32, part.shape[0] // 32, part.shape[1])
    got = lax.all_to_all(chunks, TOKENS, 0, 0)
    return jnp.sum(got.astype(F32), axis=0).astype(BF)


def other_core(value):
    return lax.ppermute(value, "gx", [(0, 1), (1, 0), (2, 3), (3, 2)])


def other_half(value):
    return lax.ppermute(value, "gx", [(0, 2), (1, 3), (2, 0), (3, 1)])


def on_device(
    block_in, online_gate, online_up, online_down, target_gate, target_up, target_down, cotangent
):
    scale_in = 1.0 / math.sqrt(D)
    scale_hid = 1.0 / math.sqrt(FF)
    core = lax.axis_index("gx") % 2
    rows_all = gather_rows(block_in)
    cot_all = gather_rows(cotangent)

    def halves(value):
        half = value.shape[0] // 2
        keep = lax.dynamic_slice_in_dim(value, core * half, half, 0)
        send = lax.dynamic_slice_in_dim(value, (1 - core) * half, half, 0)
        return keep, send

    def width_sum(keep, send):
        chip = keep + other_core(send).astype(F32)
        return chip + other_half(chip.astype(BF)).astype(F32)

    def both_halves(value):
        other = other_core(value)
        lower = jnp.where(core == 0, value, other)
        upper = jnp.where(core == 0, other, value)
        return jnp.concatenate([lower, upper], axis=0)

    rows_keep, rows_send = halves(rows_all)

    def project(gate, up):
        def both(rows):
            return jnp.concatenate(
                [
                    jnp.dot(rows, gate, preferred_element_type=F32) * scale_in,
                    jnp.dot(rows, up, preferred_element_type=F32) * scale_in,
                ],
                axis=1,
            )

        pre = width_sum(both(rows_keep), both(rows_send).astype(BF))
        return pre[:, :512], pre[:, 512:]

    tg_gate, tg_up = project(target_gate, target_up)
    on_gate, on_up = project(online_gate, online_up)
    tg_hidden = both_halves(activate(tg_gate, tg_up))
    target_out = scatter_sum(
        (jnp.dot(tg_hidden, target_down, preferred_element_type=F32) * scale_hid).astype(BF)
    )
    cot_keep, cot_send = halves(cot_all)

    def back(rows):
        return jnp.einsum("tk,fk->tf", rows, online_down, preferred_element_type=F32) * scale_hid

    hidden_grad = width_sum(back(cot_keep), back(cot_send).astype(BF))
    d_gate, d_up = hidden_grads(on_gate, on_up, hidden_grad)
    packed = both_halves(jnp.concatenate([activate(on_gate, on_up), d_gate, d_up], axis=1))
    on_hidden, d_gate, d_up = packed[:, :512], packed[:, 512:1024], packed[:, 1024:]
    online_out = scatter_sum(
        (jnp.dot(on_hidden, online_down, preferred_element_type=F32) * scale_hid).astype(BF)
    )
    summed = jnp.einsum("tf,kf->tk", d_gate, online_gate, preferred_element_type=F32)
    summed = summed + jnp.einsum("tf,kf->tk", d_up, online_up, preferred_element_type=F32)
    grad_in = scatter_sum((summed * scale_in).astype(BF))
    grad_gate = (
        jnp.einsum("tk,tf->kf", rows_all, d_gate, preferred_element_type=F32) * scale_in
    ).astype(BF)
    grad_up = (
        jnp.einsum("tk,tf->kf", rows_all, d_up, preferred_element_type=F32) * scale_in
    ).astype(BF)
    grad_down = (
        jnp.einsum("tf,tk->fk", on_hidden, cot_all, preferred_element_type=F32) * scale_hid
    ).astype(BF)
    new_gate = blend(online_gate, target_gate)
    new_up = blend(online_up, target_up)
    new_down = blend(online_down, target_down)
    return (
        online_out,
        target_out,
        grad_in,
        grad_gate,
        grad_up,
        grad_down,
        new_gate,
        new_up,
        new_down,
    )


def solution(mesh):
    tokens = P(("gy", "gz"), "gx")
    wide = P("gx", ("gy", "gz"))
    tall = P(("gy", "gz"), "gx")
    return jax.shard_map(
        on_device,
        mesh=mesh,
        in_specs=(tokens, wide, wide, tall, wide, wide, tall, tokens),
        out_specs=(tokens, tokens, tokens, wide, wide, tall, wide, wide, tall),
        check_vma=False,
    )
```

time: 1020 us -> 289 us (0.28); the launches traced: 1010 us -> 288 us
  waiting for transfers between devices: 909 us -> 122 us
  blocking collectives: 0 us -> 47.2 us
  starting transfers between devices: 0.42 us -> 31.1 us
  between operations: 14.2 us -> 1.11 us
  matrix products: 53.9 us -> 43.6 us
    reduce_scatter x3 -> x0, waiting for transfers between devices: 456 us -> none  [the longest x1 171 us: on_device(): lax.psum_scatter(summed * scale_in, ('gy', 'gz'), scatter_dimension=0, ti...]
    all_gather x2 -> x0, waiting for transfers between devices: 293 us -> none  [the longest x1 152 us: on_device(): lax.all_gather(block_in, ('gy', 'gz'), axis=0, tiled=True)]
    psum x1 -> x0, waiting for transfers between devices: 159 us -> none  [on_device(): lax.psum((partial_on_gate, partial_on_up, partial_tg_gate, partial_tg_up)...]
    all_to_all x0 -> x4, waiting for transfers between devices: none -> 88.7 us  [the longest x3 58.6 us: scatter_sum(): got = lax.all_to_all(chunks, TOKENS, 0, 0)]
    all_to_all x0 -> x1, blocking collectives: none -> 47.2 us  [gather_rows(): got = lax.all_to_all(copies, TOKENS, 0, 0)]
    ppermute x0 -> x8, waiting for transfers between devices: none -> 33.4 us  [the longest x3 30.5 us: other_half(): return lax.ppermute(value, 'gx', [(0, 2), (1, 3), (2, 0), (3, 1)])]
    all_to_all x0 -> x4, starting transfers between devices: none -> 24.8 us  [the longest x3 18.7 us: scatter_sum(): got = lax.all_to_all(chunks, TOKENS, 0, 0)]
    dot_general x12 -> x17, matrix products: 53.9 us -> 43.6 us  [the longest x2 6.67 us: back(): jnp.einsum('tk,fk->tf', rows, online_down, preferred_element_type=F32)]
  transfers between devices with their start and end apart: 6 -> 12, of which waited for: 6 -> 8; matrix products, arithmetic and copies ran while one was open for 7% -> 27% of each run, Pallas kernels for 0% -> 0%
where the time goes in v1:
time: 289 us; the launch traced here: 288 us
  waiting for transfers between devices  122 us (42%)
  blocking collectives  47.2 us (16%)
  matrix products  43.6 us (15%)
  starting transfers between devices  31.1 us (11%)
  other arithmetic  28.9 us (10%)
  local copies, waits for them, and re-layouts  13.6 us (5%)
    all_to_all x3, waiting for transfers between devices, scatter_sum(): got = lax.all_to_all(chunks, TOKENS, 0, 0)  58.6 us
    all_to_all x1, blocking collectives, gather_rows(): got = lax.all_to_all(copies, TOKENS, 0, 0)  47.2 us
    ppermute x3, waiting for transfers between devices, other_half(): return lax.ppermute(value, 'gx', [(0, 2), (1, 3), (2, 0), (3, 1)])  30.5 us
    all_to_all x1, waiting for transfers between devices, gather_rows(): got = lax.all_to_all(copies, TOKENS, 0, 0)  30.2 us
    all_to_all x3, starting transfers between devices, scatter_sum(): got = lax.all_to_all(chunks, TOKENS, 0, 0)  18.7 us
    convert_element_type x2, other arithmetic, blend(): return (target_f + POLYAK * (online_f - target_f)).astype(BF)  10 us
    unnamed x56, local copies, waits for them, and re-layouts  9.97 us
    reduce_sum x3, other arithmetic, scatter_sum(): return jnp.sum(got.astype(F32), axis=0).astype(BF)  9.39 us
  transfers between devices with their start and end apart: 12, of which 8 were waited for; matrix products, arithmetic and copies ran while one was open for 27% of the time, Pallas kernels for 0%

profile of v1, /device:TPU:10, one launch (start us, length us, event | category | flops | bytes accessed | tf_op | source)
XLA Modules:
  0.0 287.5 jit_solution(245665472925427765)
XLA Ops:
  1.9 47.2 %all_to_all.25 = bf16[32,24,2048]{2,1,0:T(8,128)(2,1)S(1)} all-to-all(bf16[32,24,2048]{2,1,0:T(8,128)(2,1)S(1)} %broadcast_in_dim.4), channel_id=1, replica_groups=mesh['gx'=4,'gy'=4,'gz'=8] {'gy','gz'}, dimensions={0} | all-to-all | bytes 6291456 | tf_op jit(solution)/shard_map/all_to_all | solution.py:37
  49.2 2.3 broadcast_in_dim.5
  51.5 6.2 %all-to-all-start.1 = ((bf16[32,24,2048]{2,1,0:T(8,128)(2,1)}), bf16[32,24,2048]{2,1,0:T(8,128)(2,1)}, u32[]{:S(2)}, u32[]{:S(2)}) async-start(bf16[32,24,2048]{2,1,0:T(8,128)(2,1)} %broadcast_in_dim.5), calls=%async_computation.1 | async-start | bytes 6291456 | tf_op jit(solution)/shard_map/all_to_all | solution.py:37
  57.7 2.7 fusion.21
  69.4 2.3 collective-permute-start.6
  71.7 30.2 %all-to-all-done.1 = bf16[32,24,2048]{2,1,0:T(8,128)(2,1)} async-done(((bf16[32,24,2048]{2,1,0:T(8,128)(2,1)}), bf16[32,24,2048]{2,1,0:T(8,128)(2,1)}, u32[]{:S(2)}, u32[]{:S(2)}) %all-to-all-start.1) | async-done | bytes 3145760 | tf_op jit(solution)/shard_map/all_to_all | solution.py:37
  101.8 3.2 %fusion.22 = bf16[384,512]{1,0:T(8,128)(2,1)S(1)} fusion(bf16[512,2048]{1,0:T(8,128)(2,1)} %param.11, bf16[768,2048]{1,0:T(8,128)(2,1)} %bitcast.1, s32[]{:T(128)S(6)} %select_n.42), kind=kOutput, calls=%fused_computation.46 | convolution fusion | flops 805699584 | bytes 4063236 | tf_op jit(solution)/shard_map/tk,fk->tf/dot_general | solution.py:104
  107.7 9.5 %collective-permute-done.6 = bf16[384,1024]{1,0:T(8,128)(2,1)} collective-permute-done((bf16[384,1024]{1,0:T(8,128)(2,1)}, bf16[384,1024]{1,0:T(8,128)(2,1)}, u32[]{:S(2)}, u32[]{:S(2)}) %collective-permute-start.6) | collective-permute-done | bytes 786464 | tf_op jit(solution)/shard_map/ppermute | solution.py:52
  122.0 3.5 %fusion.41 = (bf16[384,512]{1,0:T(8,128)(2,1)}, f32[384,512]{1,0:T(8,128)}) fusion(bf16[384,512]{1,0:T(8,128)(2,1)S(1)} %collective-permute-done.2, bf16[512,2048]{1,0:T(8,128)(2,1)S(1)} %copy-done.19, bf16[768,2048]{1,0:T(8,128)(2,1)} %bitcast.1, s32[]{:T(128)S(6)} %select_n.41), kind=kOutput, calls=%fused_computation.76 | convolution fusion | flops 806092800 | bytes 5242884 | tf_op jit(solution)/shard_map/tk,fk->tf/dot_general | solution.py:104
  128.2 3.5 %multiply_convert_fusion.1 = bf16[768,2048]{1,0:T(8,128)(2,1)} fusion(bf16[512,2048]{1,0:T(8,128)(2,1)S(1)} %copy-done.21, bf16[384,512]{1,0:T(8,128)(2,1)S(1)} %get-tuple-element.24, bf16[384,512]{1,0:T(8,128)(2,1)S(1)} %get-tuple-element.23), kind=kOutput, calls=%fused_computation.1 | convolution fusion | flops 1615331328 | bytes 6029312 | tf_op jit(solution)/shard_map/dot_general | solution.py:99
  131.7 6.5 %all-to-all-start.3 = ((bf16[32,24,2048]{2,1,0:T(8,128)(2,1)}), bf16[32,24,2048]{2,1,0:T(8,128)(2,1)}, u32[]{:S(2)}, u32[]{:S(2)}) async-start(bf16[32,24,2048]{2,1,0:T(8,128)(2,1)} %bitcast.3), calls=%async_computation.3 | async-start | bytes 6291456 | tf_op jit(solution)/shard_map/all_to_all | solution.py:43
  138.2 12.2 %collective-permute-done.1 = bf16[384,1024]{1,0:T(8,128)(2,1)S(1)} collective-permute-done((bf16[384,1024]{1,0:T(8,128)(2,1)S(1)}, bf16[384,1024]{1,0:T(8,128)(2,1)S(1)}, u32[]{:S(2)}, u32[]{:S(2)}) %collective-permute-start.1) | collective-permute-done | bytes 786464 | tf_op jit(solution)/shard_map/ppermute | solution.py:52
  151.9 8.8 %collective-permute-done.3 = bf16[384,512]{1,0:T(8,128)(2,1)} collective-permute-done((bf16[384,512]{1,0:T(8,128)(2,1)}, bf16[384,512]{1,0:T(8,128)(2,1)}, u32[]{:S(2)}, u32[]{:S(2)}) %collective-permute-start.3) | collective-permute-done | bytes 393248 | tf_op jit(solution)/shard_map/ppermute | solution.py:52
  162.4 2.8 collective-permute-done.4
  165.7 3.5 %multiply_convert_fusion.2 = bf16[768,2048]{1,0:T(8,128)(2,1)} fusion(bf16[512,2048]{1,0:T(8,128)(2,1)S(1)} %copy-done.20, bf16[384,1536]{1,0:T(8,128)(2,1)S(1)} %get-tuple-element.21, bf16[384,1536]{1,0:T(8,128)(2,1)S(1)} %get-tuple-element.20), kind=kOutput, calls=%fused_computation.2 | convolution fusion | flops 1615331328 | bytes 7602176 | tf_op jit(solution)/shard_map/dot_general | solution.py:111
  169.2 13.9 %all-to-all-done.3 = bf16[32,24,2048]{2,1,0:T(8,128)(2,1)} async-done(((bf16[32,24,2048]{2,1,0:T(8,128)(2,1)}), bf16[32,24,2048]{2,1,0:T(8,128)(2,1)}, u32[]{:S(2)}, u32[]{:S(2)}) %all-to-all-start.3) | async-done | bytes 3145760 | tf_op jit(solution)/shard_map/all_to_all | solution.py:43
  183.1 6.9 %all-to-all-start.2 = ((bf16[32,24,2048]{2,1,0:T(8,128)(2,1)}), bf16[32,24,2048]{2,1,0:T(8,128)(2,1)}, u32[]{:S(2)}, u32[]{:S(2)}) async-start(bf16[32,24,2048]{2,1,0:T(8,128)(2,1)} %bitcast.37), calls=%async_computation.2 | async-start | bytes 6291456 | tf_op jit(solution)/shard_map/all_to_all | solution.py:43
  190.0 3.6 %fusion.53 = f32[768,2048]{1,0:T(8,128)S(1)} fusion(bf16[2048,512]{1,0:T(8,128)(2,1)} %param.10, bf16[384,1536]{1,0:T(8,128)(2,1)S(1)} %get-tuple-element.20, bf16[384,1536]{1,0:T(8,128)(2,1)S(1)} %get-tuple-element.21), kind=kOutput, calls=%fused_computation.90 | convolution fusion | flops 1612185600 | bytes 10747904 | tf_op jit(solution)/shard_map/tf,kf->tk/dot_general | solution.py:114
  193.6 3.5 %multiply_convert_fusion = bf16[768,2048]{1,0:T(8,128)(2,1)} fusion(f32[768,2048]{1,0:T(8,128)S(1)} %fusion.53, bf16[2048,512]{1,0:T(8,128)(2,1)S(1)} %copy-done.7, bf16[384,1536]{1,0:T(8,128)(2,1)S(1)} %get-tuple-element.21, bf16[384,1536]{1,0:T(8,128)(2,1)S(1)} %get-tuple-element.20), kind=kOutput, calls=%fused_computation | convolution fusion | flops 1616904192 | bytes 13893632 | tf_op jit(solution)/shard_map/tf,kf->tk/dot_general | solution.py:113
  197.1 37.0 %all-to-all-done.2 = bf16[32,24,2048]{2,1,0:T(8,128)(2,1)} async-done(((bf16[32,24,2048]{2,1,0:T(8,128)(2,1)}), bf16[32,24,2048]{2,1,0:T(8,128)(2,1)}, u32[]{:S(2)}, u32[]{:S(2)}) %all-to-all-start.2) | async-done | bytes 3145760 | tf_op jit(solution)/shard_map/all_to_all | solution.py:43
  234.1 5.2 %all-to-all-start.4 = ((bf16[32,24,2048]{2,1,0:T(8,128)(2,1)}), bf16[32,24,2048]{2,1,0:T(8,128)(2,1)}, u32[]{:S(2)}, u32[]{:S(2)}) async-start(bf16[32,24,2048]{2,1,0:T(8,128)(2,1)} %bitcast.36), calls=%async_computation.4 | async-start | bytes 6291456 | tf_op jit(solution)/shard_map/all_to_all | solution.py:43
  239.3 4.7 %fusion.5 = bf16[512,2048]{1,0:T(8,128)(2,1)} fusion(bf16[512,2048]{1,0:T(8,128)(2,1)} %param.14, bf16[512,2048]{1,0:T(8,128)(2,1)} %param.11), kind=kLoop, calls=%fused_computation.14 | loop fusion | flops 6291456 | bytes 6291456 | tf_op jit(solution)/shard_map/convert_element_type | solution.py:32
  244.1 5.3 %fusion.1 = (bf16[2048,512]{1,0:T(8,128)(2,1)}, bf16[2048,512]{1,0:T(8,128)(2,1)}) fusion(bf16[2048,512]{1,0:T(8,128)(2,1)} %param.12, bf16[2048,512]{1,0:T(8,128)(2,1)S(1)} %copy-done.8, bf16[2048,512]{1,0:T(8,128)(2,1)S(1)} %copy-done.4, bf16[2048,512]{1,0:T(8,128)(2,1)S(1)} %copy-done.23), kind=kLoop, calls=%fused_computation.10 | loop fusion | flops 12582912 | bytes 12582912 | tf_op jit(solution)/shard_map/convert_element_type | solution.py:32
  249.4 3.2 %fusion.6 = bf16[2048,512]{0,1:T(8,128)(2,1)} fusion(bf16[768,2048]{1,0:T(8,128)(2,1)S(1)} %bitcast.35, bf16[384,1536]{1,0:T(8,128)(2,1)S(1)} %get-tuple-element.21, bf16[384,1536]{1,0:T(8,128)(2,1)S(1)} %get-tuple-element.20), kind=kOutput, calls=%fused_computation.18 | convolution fusion | flops 1614282752 | bytes 7602176 | tf_op jit(solution)/shard_map/tk,tf->kf/dot_general | solution.py:117
  252.6 3.9 %copy.17 = bf16[2048,512]{1,0:T(8,128)(2,1)} copy(bf16[2048,512]{0,1:T(8,128)(2,1)} %fusion.6) | data formatting | bytes 4194304
  256.5 5.0 %fusion.7 = bf16[2048,512]{0,1:T(8,128)(2,1)} fusion(bf16[768,2048]{1,0:T(8,128)(2,1)} %bitcast.34, bf16[384,1536]{1,0:T(8,128)(2,1)S(1)} %get-tuple-element.20, bf16[384,1536]{1,0:T(8,128)(2,1)S(1)} %get-tuple-element.21), kind=kOutput, calls=%fused_computation.19 | convolution fusion | flops 1614282752 | bytes 7602176 | tf_op jit(solution)/shard_map/tk,tf->kf/dot_general | solution.py:120
  261.5 3.9 %copy.18 = bf16[2048,512]{1,0:T(8,128)(2,1)} copy(bf16[2048,512]{0,1:T(8,128)(2,1)} %fusion.7) | data formatting | bytes 4194304
  265.4 5.0 %multiply_convert_fusion.3 = bf16[512,2048]{1,0:T(8,128)(2,1)} fusion(bf16[768,2048]{1,0:T(8,128)(2,1)} %bitcast.1, bf16[384,1536]{1,0:T(8,128)(2,1)S(1)} %get-tuple-element.21, bf16[384,1536]{1,0:T(8,128)(2,1)S(1)} %get-tuple-element.20), kind=kOutput, calls=%fused_computation.15 | convolution fusion | flops 1614282752 | bytes 7602176 | tf_op jit(solution)/shard_map/tf,tk->fk/dot_general | solution.py:123
  270.5 3.1 %reduce_sum.37 = bf16[24,2048]{1,0:T(8,128)(2,1)} reduce(bf16[32,24,2048]{2,1,0:T(8,128)(2,1)} %all-to-all-done.3, bf16[]{:T(256)} %constant.44.clone.1), dimensions={0}, to_apply=%region_1.2 | reduce | flops 1523712 | bytes 3244034 | tf_op jit(solution)/shard_map/reduce_sum | solution.py:44
  273.6 3.1 %reduce_sum.36 = bf16[24,2048]{1,0:T(8,128)(2,1)} reduce(bf16[32,24,2048]{2,1,0:T(8,128)(2,1)} %all-to-all-done.2, bf16[]{:T(256)} %constant.44.clone.1), dimensions={0}, to_apply=%region_0.1 | reduce | flops 1523712 | bytes 3244034 | tf_op jit(solution)/shard_map/reduce_sum | solution.py:44
  276.7 7.7 %all-to-all-done.4 = bf16[32,24,2048]{2,1,0:T(8,128)(2,1)} async-done(((bf16[32,24,2048]{2,1,0:T(8,128)(2,1)}), bf16[32,24,2048]{2,1,0:T(8,128)(2,1)}, u32[]{:S(2)}, u32[]{:S(2)}) %all-to-all-start.4) | async-done | bytes 3145760 | tf_op jit(solution)/shard_map/all_to_all | solution.py:43
  284.4 3.1 %reduce_sum.38 = bf16[24,2048]{1,0:T(8,128)(2,1)} reduce(bf16[32,24,2048]{2,1,0:T(8,128)(2,1)} %all-to-all-done.4, bf16[]{:T(256)} %constant.44.clone.1), dimensions={0}, to_apply=%region_2.3 | reduce | flops 1523712 | bytes 3244034 | tf_op jit(solution)/shard_map/reduce_sum | solution.py:44
  (84 shorter events, 23.8 us)
Async XLA Ops:
  1.9 47.3 %copy-start.26 = (bf16[24,2048]{1,0:T(8,128)(2,1)S(1)}, bf16[24,2048]{1,0:T(8,128)(2,1)}, u32[]{:S(2)}) copy-start(bf16[24,2048]{1,0:T(8,128)(2,1)} %param.15) | copy-start | bytes 294916
  49.2 57.0 %copy-start = (bf16[32,24,2048]{2,1,0:T(8,128)(2,1)}, bf16[32,24,2048]{2,1,0:T(8,128)(2,1)S(1)}, u32[]{:S(2)}) copy-start(bf16[32,24,2048]{2,1,0:T(8,128)(2,1)S(1)} %all_to_all.25) | copy-start | bytes 9437188
  51.5 50.3 %all-to-all-start.1 = ((bf16[32,24,2048]{2,1,0:T(8,128)(2,1)}), bf16[32,24,2048]{2,1,0:T(8,128)(2,1)}, u32[]{:S(2)}, u32[]{:S(2)}) async-start(bf16[32,24,2048]{2,1,0:T(8,128)(2,1)} %broadcast_in_dim.5), calls=%async_computation.1 | async-start | bytes 6291456 | tf_op jit(solution)/shard_map/all_to_all | solution.py:37
  57.7 2.7 copy-start.24
  61.6 5.7 %collective-permute-start.5 = (bf16[384,1024]{1,0:T(8,128)(2,1)S(1)}, bf16[384,1024]{1,0:T(8,128)(2,1)S(1)}, u32[]{:S(2)}, u32[]{:S(2)}) collective-permute-start(bf16[384,1024]{1,0:T(8,128)(2,1)S(1)} %pad_maximum_fusion.3), channel_id=1, source_target_pairs={{0,32},{32,0},{64,96},{96,64},{1,33},{33,1},{65,97},{97,65},{2,34}... | collective-permute-start | bytes 2359304 | tf_op jit(solution)/shard_map/ppermute | solution.py:48
  65.3 53.8 %collective-permute-start = (bf16[384,1024]{1,0:T(8,128)(2,1)}, bf16[384,1024]{1,0:T(8,128)(2,1)}, u32[]{:S(2)}, u32[]{:S(2)}) collective-permute-start(bf16[384,1024]{1,0:T(8,128)(2,1)} %pad_maximum_fusion.2), channel_id=1, source_target_pairs={{0,32},{32,0},{64,96},{96,64},{1,33},{33,1},{65,97},{97,65},{2,34}... | collective-permute-start | bytes 2359304 | tf_op jit(solution)/shard_map/ppermute | solution.py:48
  69.4 47.8 %collective-permute-start.6 = (bf16[384,1024]{1,0:T(8,128)(2,1)}, bf16[384,1024]{1,0:T(8,128)(2,1)}, u32[]{:S(2)}, u32[]{:S(2)}) collective-permute-start(bf16[384,1024]{1,0:T(8,128)(2,1)} %fusion.33), channel_id=1, source_target_pairs={{0,64},{32,96},{64,0},{96,32},{1,65},{33,97},{65,1},{97,33},{2,66}... | collective-permute-start | bytes 2359304 | tf_op jit(solution)/shard_map/ppermute | solution.py:52
  101.8 3.3 %copy-start.3 = (bf16[2048,512]{1,0:T(8,128)(2,1)S(1)}, bf16[2048,512]{1,0:T(8,128)(2,1)}, u32[]{:S(2)}) copy-start(bf16[2048,512]{1,0:T(8,128)(2,1)} %param.10) | copy-start | bytes 6291460
  105.1 17.0 %collective-permute-start.2 = (bf16[384,512]{1,0:T(8,128)(2,1)S(1)}, bf16[384,512]{1,0:T(8,128)(2,1)S(1)}, u32[]{:S(2)}, u32[]{:S(2)}) collective-permute-start(bf16[384,512]{1,0:T(8,128)(2,1)S(1)} %fusion.22), channel_id=1, source_target_pairs={{0,32},{32,0},{64,96},{96,64},{1,33},{33,1},{65,97},{97,65},{2,34}... | collective-permute-start | bytes 1179656 | tf_op jit(solution)/shard_map/ppermute | solution.py:48
  106.7 12.4 %copy-start.9 = (f32[384,512]{1,0:T(8,128)}, f32[384,512]{1,0:T(8,128)S(1)}, u32[]{:S(2)}) copy-start(f32[384,512]{1,0:T(8,128)S(1)} %convolution_multiply_fusion.6) | copy-start | bytes 2359300
  106.7 10.5 %copy-start.14 = (bf16[384,1024]{1,0:T(8,128)(2,1)S(1)}, bf16[384,1024]{1,0:T(8,128)(2,1)}, u32[]{:S(2)}) copy-start(bf16[384,1024]{1,0:T(8,128)(2,1)} %copy-done.13) | copy-start | bytes 2359300
  106.7 10.5 %copy-start.16 = (f32[384,512]{1,0:T(8,128)S(1)}, f32[384,512]{1,0:T(8,128)}, u32[]{:S(2)}) copy-start(f32[384,512]{1,0:T(8,128)} %copy-done.15) | copy-start | bytes 2359300
  106.7 10.5 %copy-start.18 = (f32[384,512]{1,0:T(8,128)S(1)}, f32[384,512]{1,0:T(8,128)}, u32[]{:S(2)}) copy-start(f32[384,512]{1,0:T(8,128)} %copy-done.17) | copy-start | bytes 2359300
  107.7 11.4 %copy-start.11 = (f32[384,512]{1,0:T(8,128)}, f32[384,512]{1,0:T(8,128)S(1)}, u32[]{:S(2)}) copy-start(f32[384,512]{1,0:T(8,128)S(1)} %convolution_multiply_fusion.7) | copy-start | bytes 2359300
  118.7 3.3 %copy-start.19 = (bf16[512,2048]{1,0:T(8,128)(2,1)S(1)}, bf16[512,2048]{1,0:T(8,128)(2,1)}, u32[]{:S(2)}) copy-start(bf16[512,2048]{1,0:T(8,128)(2,1)} %param.11) | copy-start | bytes 6291460
  119.0 8.8 %collective-permute-start.7 = (bf16[384,512]{1,0:T(8,128)(2,1)S(1)}, bf16[384,512]{1,0:T(8,128)(2,1)S(1)}, u32[]{:S(2)}, u32[]{:S(2)}) collective-permute-start(bf16[384,512]{1,0:T(8,128)(2,1)S(1)} %fusion.37), channel_id=1, source_target_pairs={{0,32},{32,0},{64,96},{96,64},{1,33},{33,1},{65,97},{97,65},{2,34}... | collective-permute-start | bytes 1179656 | tf_op jit(solution)/shard_map/ppermute | solution.py:48
  120.7 29.7 %collective-permute-start.1 = (bf16[384,1024]{1,0:T(8,128)(2,1)S(1)}, bf16[384,1024]{1,0:T(8,128)(2,1)S(1)}, u32[]{:S(2)}, u32[]{:S(2)}) collective-permute-start(bf16[384,1024]{1,0:T(8,128)(2,1)S(1)} %fusion.34), channel_id=1, source_target_pairs={{0,64},{32,96},{64,0},{96,32},{1,65},{33,97},{65,1},{97,33},{2,66}... | collective-permute-start | bytes 2359304 | tf_op jit(solution)/shard_map/ppermute | solution.py:52
  125.5 2.7 copy-start.21
  125.5 35.2 %collective-permute-start.3 = (bf16[384,512]{1,0:T(8,128)(2,1)}, bf16[384,512]{1,0:T(8,128)(2,1)}, u32[]{:S(2)}, u32[]{:S(2)}) collective-permute-start(bf16[384,512]{1,0:T(8,128)(2,1)} %get-tuple-element.25), channel_id=1, source_target_pairs={{0,64},{32,96},{64,0},{96,32},{1,65},{33,97},{65,1},{97,33},{2,66}... | collective-permute-start | bytes 1179656 | tf_op jit(solution)/shard_map/ppermute | solution.py:52
  131.7 18.8 %copy-start.10 = (f32[384,512]{1,0:T(8,128)S(1)}, f32[384,512]{1,0:T(8,128)}, u32[]{:S(2)}) copy-start(f32[384,512]{1,0:T(8,128)} %copy-done.9) | copy-start | bytes 2359300
  131.7 18.8 %copy-start.12 = (f32[384,512]{1,0:T(8,128)S(1)}, f32[384,512]{1,0:T(8,128)}, u32[]{:S(2)}) copy-start(f32[384,512]{1,0:T(8,128)} %copy-done.11) | copy-start | bytes 2359300
  131.7 51.4 %all-to-all-start.3 = ((bf16[32,24,2048]{2,1,0:T(8,128)(2,1)}), bf16[32,24,2048]{2,1,0:T(8,128)(2,1)}, u32[]{:S(2)}, u32[]{:S(2)}) async-start(bf16[32,24,2048]{2,1,0:T(8,128)(2,1)} %bitcast.3), calls=%async_computation.3 | async-start | bytes 6291456 | tf_op jit(solution)/shard_map/all_to_all | solution.py:43
  138.2 22.5 %copy-start.25 = (f32[384,512]{1,0:T(8,128)S(1)}, f32[384,512]{1,0:T(8,128)}, u32[]{:S(2)}) copy-start(f32[384,512]{1,0:T(8,128)} %get-tuple-element.26) | copy-start | bytes 2359300
  162.3 3.4 %copy-start.20 = (bf16[512,2048]{1,0:T(8,128)(2,1)S(1)}, bf16[512,2048]{1,0:T(8,128)(2,1)}, u32[]{:S(2)}) copy-start(bf16[512,2048]{1,0:T(8,128)(2,1)} %param.11) | copy-start | bytes 6291460
  162.3 2.9 %collective-permute-start.4 = (bf16[384,1536]{1,0:T(8,128)(2,1)S(1)}, bf16[384,1536]{1,0:T(8,128)(2,1)S(1)}, u32[]{:S(2)}, u32[]{:S(2)}) collective-permute-start(bf16[384,1536]{1,0:T(8,128)(2,1)S(1)} %pad_maximum_fusion), channel_id=1, source_target_pairs={{0,32},{32,0},{64,96},{96,64},{1,33},{33,1},{65,97},{97,65},{2,34}... | collective-permute-start | bytes 3538952 | tf_op jit(solution)/shard_map/ppermute | solution.py:48
  183.1 51.0 %all-to-all-start.2 = ((bf16[32,24,2048]{2,1,0:T(8,128)(2,1)}), bf16[32,24,2048]{2,1,0:T(8,128)(2,1)}, u32[]{:S(2)}, u32[]{:S(2)}) async-start(bf16[32,24,2048]{2,1,0:T(8,128)(2,1)} %bitcast.37), calls=%async_computation.2 | async-start | bytes 6291456 | tf_op jit(solution)/shard_map/all_to_all | solution.py:43
  190.0 3.6 %copy-start.7 = (bf16[2048,512]{1,0:T(8,128)(2,1)S(1)}, bf16[2048,512]{1,0:T(8,128)(2,1)}, u32[]{:S(2)}) copy-start(bf16[2048,512]{1,0:T(8,128)(2,1)} %param.9) | copy-start | bytes 6291460
  234.1 50.4 %all-to-all-start.4 = ((bf16[32,24,2048]{2,1,0:T(8,128)(2,1)}), bf16[32,24,2048]{2,1,0:T(8,128)(2,1)}, u32[]{:S(2)}, u32[]{:S(2)}) async-start(bf16[32,24,2048]{2,1,0:T(8,128)(2,1)} %bitcast.36), calls=%async_computation.4 | async-start | bytes 6291456 | tf_op jit(solution)/shard_map/all_to_all | solution.py:43
  239.3 4.8 %copy-start.4 = (bf16[2048,512]{1,0:T(8,128)(2,1)S(1)}, bf16[2048,512]{1,0:T(8,128)(2,1)}, u32[]{:S(2)}) copy-start(bf16[2048,512]{1,0:T(8,128)(2,1)} %param.10) | copy-start | bytes 6291460
  239.3 4.8 %copy-start.8 = (bf16[2048,512]{1,0:T(8,128)(2,1)S(1)}, bf16[2048,512]{1,0:T(8,128)(2,1)}, u32[]{:S(2)}) copy-start(bf16[2048,512]{1,0:T(8,128)(2,1)} %param.9) | copy-start | bytes 6291460
  239.3 4.8 %copy-start.23 = (bf16[2048,512]{1,0:T(8,128)(2,1)S(1)}, bf16[2048,512]{1,0:T(8,128)(2,1)}, u32[]{:S(2)}) copy-start(bf16[2048,512]{1,0:T(8,128)(2,1)} %param.13) | copy-start | bytes 6291460
  244.1 5.3 %copy-start.1 = (bf16[32,24,2048]{2,1,0:T(8,128)(2,1)S(1)}, bf16[32,24,2048]{2,1,0:T(8,128)(2,1)}, u32[]{:S(2)}) copy-start(bf16[32,24,2048]{2,1,0:T(8,128)(2,1)} %copy-done) | copy-start | bytes 9437188
  (7 other events, 10.9 us)
